TPU v7x, 32 devices: a whole 2x2x4 slice. The times are simulated.
32 devices in a mesh: feat: 8 (over y, x, core), batch: 4 (over z).
Axes of the slice: x: 2, y: 2, z: 4, core: 2. Of those that a mesh axis runs over, the one named last changes fastest.
Arguments:
- features: bfloat16 [32768, 4096], P('batch', 'feat'), may hold values from -6 to 6
- src_tile: int32 [32, 2], P('batch'), may hold values from 0 to 7
- rel_type: int32 [32, 2], P('batch'), may hold values from 0 to 3
- timestamps: int32 [4096], P(('batch', 'feat')), may hold values from 0 to 127
- edge_tiles: bfloat16 [4, 128, 1024], replicated, may hold values from -0.1875 to 0.1875
- rel_weight: bfloat16 [4, 4096, 512], P(None, 'feat'), may hold values from -0.09375 to 0.09375
- attn_gain: float32 [512], replicated, may hold values from 0.1 to 1.9
- w_qkv: bfloat16 [512, 1536], replicated, as said below
- w_out: bfloat16 [512, 512], replicated, may hold values from -0.25 to 0.25
- cotangent: bfloat16 [4096, 512], P(('batch', 'feat')), may hold values from -96 to 96
Outputs:
- layer_out: bfloat16 [4096, 512], P(('batch', 'feat'))
- grad_qkv: bfloat16 [512, 1536], replicated
- grad_out: bfloat16 [512, 512], replicated
- grad_gain: bfloat16 [512], replicated
- grad_rel: bfloat16 [4, 4096, 512], P(None, 'feat')
Inputs may be any that keep to these rules, and one draw needn't show every extreme that they name: `src_tile`: index of a source tile within the batch group. `w_qkv`: query, key and value columns in that order along the second dimension.
All inputs are finite; a program needn't handle non-finite values.
Results may differ from a plain program's by a relative error of at most 0.014.
Values may be sent and summed in bfloat16 or wider, within the bound.
A program may use at most 128 MiB of HBM per device.

v0:
```python
import math

import jax
import jax.numpy as jnp
from jax import lax
from jax.sharding import PartitionSpec as P

D = 512
HEADS = 8
HEAD_DIM = 64
NREL = 4
SLOTS = 2
SBLK = 1024


EPS = 1e-06


def aggregate(feats, sources_all, kinds_all, edge_tiles):

    def one_block(pair):
        sources, kinds = pair
        parts = []
        for slot in range(SLOTS):
            piece = lax.dynamic_slice_in_dim(feats, sources[slot] * SBLK, SBLK, 0)
            tile = lax.dynamic_index_in_dim(edge_tiles, kinds[slot], 0, keepdims=False)
            parts.append(jnp.dot(tile, piece, preferred_element_type=jnp.float32))
        member = (kinds[:, None] == jnp.arange(NREL, dtype=jnp.int32)[None, :]).astype(jnp.float32)
        merged = member[0][:, None, None] * parts[0][None]
        slot = 1
        merged = merged + member[slot][:, None, None] * parts[slot][None]
        return merged.astype(jnp.bfloat16)

    blocks = lax.map(one_block, (sources_all, kinds_all))
    return jnp.moveaxis(blocks, 1, 0).reshape(NREL, -1, feats.shape[1])


def layer_forward(tokens, gain, w_qkv, w_out, times):
    token_values = tokens.astype(jnp.float32)
    scale = lax.rsqrt(jnp.mean(token_values * token_values, axis=-1, keepdims=True) + EPS)
    normed = (token_values * scale * gain).astype(jnp.bfloat16)
    projected = jnp.dot(normed, w_qkv, preferred_element_type=jnp.float32).astype(jnp.bfloat16)
    length = tokens.shape[0]
    queries = projected[:, :D].reshape(length, HEADS, HEAD_DIM)
    keys = projected[:, D : 2 * D].reshape(length, HEADS, HEAD_DIM)
    contents = projected[:, 2 * D :].reshape(length, HEADS, HEAD_DIM)
    scores = jnp.einsum(
        "qhd,khd->hqk", queries, keys, preferred_element_type=jnp.float32
    ) / math.sqrt(HEAD_DIM)
    allowed = times[None, :] <= times[:, None]
    scores = jnp.where(allowed[None], scores, -1e30)
    weights = jax.nn.softmax(scores, axis=-1).astype(jnp.bfloat16)
    context = jnp.einsum("hqk,khd->qhd", weights, contents, preferred_element_type=jnp.float32)
    context = context.astype(jnp.bfloat16).reshape(length, D)
    return (token_values + jnp.dot(context, w_out, preferred_element_type=jnp.float32)).astype(
        jnp.bfloat16
    )


def silu_slope(total):
    sigma = jax.nn.sigmoid(total)
    return sigma * (1.0 + total * (1.0 - sigma))


def project_one(relations, rel_weight, relation, start, count):
    rows_part = lax.dynamic_slice_in_dim(relations[relation], start, count, 0)
    return jnp.dot(rows_part, rel_weight[relation], preferred_element_type=jnp.float32)


def project_every(relations, rel_weight, start, count):
    summed = project_one(relations, rel_weight, 0, start, count)
    for relation in range(1, NREL):
        summed = summed + project_one(relations, rel_weight, relation, start, count)
    return summed


def shards(
    features,
    src_tile,
    rel_type,
    timestamps,
    edge_tiles,
    rel_weight,
    attn_gain,
    w_qkv,
    w_out,
    cotangent,
):
    relations = aggregate(features, src_tile, rel_type, edge_tiles)
    own_rows = timestamps.shape[0]
    total = lax.psum_scatter(
        project_every(relations, rel_weight, jnp.int32(0), own_rows * lax.axis_size("feat")),
        "feat",
        scatter_dimension=0,
        tiled=True,
    )
    hidden = jax.nn.silu(total).astype(jnp.bfloat16)
    layer_out, pullback = jax.vjp(
        lambda a, b, c, d: layer_forward(a, b, c, d, timestamps), hidden, attn_gain, w_qkv, w_out
    )
    d_hidden, d_gain, d_qkv, d_out = pullback(cotangent)
    d_total = (d_hidden.astype(jnp.float32) * silu_slope(total)).astype(jnp.bfloat16)
    piece = lax.all_gather(d_total, "feat", axis=0, tiled=True)
    columns = lax.slice_in_dim(relations, 0, piece.shape[0], axis=1)
    rel_terms = lax.dot_general(
        columns, piece, (((1,), (0,)), ((), ())), preferred_element_type=jnp.float32
    )
    grad_rel = lax.psum(rel_terms, "batch").astype(jnp.bfloat16)
    terms = (d_qkv.astype(jnp.float32), d_out.astype(jnp.float32), d_gain)
    sums = lax.psum((terms[0], terms[1], terms[2]), ("feat", "batch"))
    grad_qkv = sums[0].astype(jnp.bfloat16)
    grad_out = sums[1].astype(jnp.bfloat16)
    grad_gain = sums[2].astype(jnp.bfloat16)
    return (layer_out, grad_qkv, grad_out, grad_gain, grad_rel)


def solution(mesh):
    in_specs = (
        P("batch", "feat"),
        P("batch", None),
        P("batch", None),
        P(("batch", "feat")),
        P(),
        P(None, "feat", None),
        P(),
        P(),
        P(),
        P(("batch", "feat"), None),
    )
    out_specs = (P(("batch", "feat"), None), P(), P(), P(), P(None, "feat", None))
    return jax.shard_map(shards, mesh=mesh, in_specs=in_specs, out_specs=out_specs, check_vma=False)
```

profile of v0, /device:TPU:1, one launch (start us, length us, event | category | flops | bytes accessed | tf_op | source)
XLA Modules:
  0.0 422.5 jit_solution(4557252624058516471)
XLA Ops:
  8.1 91.3 %while.10 = (s32[]{:T(128)}, bf16[8,4,128,512]{3,2,0,1:T(8,128)(2,1)}, s32[8,2]{1,0:T(8,128)S(1)}, bf16[4,128,1024]{2,1,0:T(8,128)(2,1)}, s32[8,2]{0,1:T(2,128)}...) while((s32[]{:T(128)}, ...), condition=%wide.region_1.2_spmd, body=%wide.region_0.1_spmd.sunk | while | flops 269484032 | bytes 4194829 | solution.py:34
  15.2 1.6 fusion.100
  16.9 1.6 fusion.102
  26.7 1.6 fusion.100
  28.3 1.6 fusion.102
  39.7 1.6 fusion.102
  49.5 1.6 fusion.100
  51.1 1.6 fusion.102
  60.9 1.6 fusion.100
  62.5 1.6 fusion.102
  72.3 1.6 fusion.100
  73.9 1.6 fusion.102
  85.3 1.6 fusion.102
  95.1 1.6 fusion.100
  96.7 1.6 fusion.102
  99.4 2.7 fusion.51
  104.4 2.0 add_add_fusion
  108.0 41.9 %reduce-scatter.2.cloned.1.call-done = f32[128,512]{1,0:T(8,128)} async-done(((f32[1024,512]{1,0:T(8,128)}), f32[128,512]{1,0:T(8,128)}) %reduce-scatter.2.cloned.1.call-update) | async-done | bytes 262160 | tf_op jit(solution)/shard_map/reduce_scatter | solution.py:91
  155.5 1.7 convolution_convert_fusion.4
  157.2 1.6 convolution_convert_fusion.5
  161.1 3.4 fusion.13
  165.4 101.0 %all-reduce.7 = (bf16[512,1536]{1,0:T(8,128)(2,1)}, bf16[512,512]{1,0:T(8,128)(2,1)}, bf16[512]{0:T(512)(128)(2,1)}) all-reduce(f32[512,1536]{1,0:T(8,128)} %fusion.13, f32[512,512]{1,0:T(8,128)S(1)} %fusion.15, f32[512]{0:T(512)S(1)} %get-tuple-element.51), channel_id=1, replica_groups=mesh['feat'=8,'batch'=4] {'feat','batch'}, use_global_device_ids=true, to_apply=%region_7.8 | all-reduce | flops 1049088 | bytes 6294528 | tf_op jit(solution)/shard_map/psum | solution.py:110
  266.3 6.8 %fusion.21 = f32[4,512,512]{2,1,0:T(8,128)} fusion(bf16[4,1024,512]{2,1,0:T(8,128)(2,1)} %bitcast.108, bf16[1024,512]{1,0:T(8,128)(2,1)} %all-gather.2.cloned.1.call-done), kind=kOutput, calls=%fused_computation.40 | convolution fusion | flops 2147483648 | bytes 9437184 | tf_op jit(solution)/shard_map/dot_general | solution.py:105
  273.1 142.5 %all-reduce.6 = bf16[4,512,512]{2,1,0:T(8,128)(2,1)} all-reduce(f32[4,512,512]{2,1,0:T(8,128)} %fusion.21), channel_id=1, replica_groups=mesh['feat'=8,'batch'=4] {'batch'}, use_global_device_ids=true, to_apply=%region_12.13 | all-reduce | flops 1048576 | bytes 6291456 | tf_op jit(solution)/shard_map/psum | solution.py:108
  (129 shorter events, 40.1 us)
Async XLA Ops:
  7.2 143.8 %copy-start = (bf16[512,1536]{1,0:T(8,128)(2,1)S(1)}, bf16[512,1536]{1,0:T(8,128)(2,1)}, u32[]{:S(2)}) copy-start(bf16[512,1536]{1,0:T(8,128)(2,1)} %param.19) | copy-start | bytes 4718596
  7.2 142.7 %reduce-scatter.2.cloned.1.call-start = ((), (), s32[]{:S(2)}) async-start(), calls=%async_computation.1 | async-start | bytes 2359296 | tf_op jit(solution)/shard_map/reduce_scatter | solution.py:91
  99.4 2.9 copy-start.1
  106.4 1.0 copy-start.2
  106.4 1.1 copy-start.3
  106.4 1.5 copy-start.13
  106.4 44.6 %copy-start.11 = (f32[512]{0:T(512)S(1)}, f32[512]{0:T(512)}, u32[]{:S(2)}) copy-start(f32[512]{0:T(512)} %param.18) | copy-start | bytes 6148
  106.4 159.9 %all-gather.2.cloned.1.call-start = ((), (), s32[]{:S(2)}) async-start(), calls=%async_computation.2 | async-start | bytes 1179648 | tf_op jit(solution)/shard_map/all_gather | solution.py:103
  108.0 45.6 %copy-start.12 = (pred[128,128]{0,1:T(8,128)(4,1)}, pred[128,128]{0,1:T(8,128)(4,1)S(1)}, u32[]{:S(2)}) copy-start(pred[128,128]{0,1:T(8,128)(4,1)S(1)} %broadcast_compare_fusion) | copy-start | bytes 49156
  151.0 2.1 copy-start.14
  151.6 2.0 copy-start.8
  151.7 2.4 copy-start.10
  154.1 4.8 %copy-start.5 = (bf16[8,64,128]{2,1,0:T(8,128)(2,1)}, bf16[8,64,128]{2,1,0:T(8,128)(2,1)S(1)}, u32[]{:S(2)}) copy-start(bf16[8,64,128]{2,1,0:T(8,128)(2,1)S(1)} %convolution_convert_fusion.6) | copy-start | bytes 393220
  155.5 1.7 copy-start.9
  157.2 2.4 copy-start.6
  158.9 1.9 copy-start.7
  158.9 0.8 copy-start.15
  158.9 1.0 copy-start.4
Sparse Core Ops, SparseCore 0:
  106.5 43.2 reduce-scatter.1
  160.9 28.1 all-gather.1
where the time goes:
time: 428 us; the launch traced here: 422 us
  blocking collectives  243 us (57%)
  matrix products  49.8 us (12%)
  waiting for transfers between devices  41.9 us (10%)
  loops' own time  41.7 us (10%)
  local copies, waits for them, and re-layouts  20.5 us (5%)
  between operations  14.3 us (3%)
  other arithmetic  10.7 us (2%)
    psum x1, blocking collectives, shards(): grad_rel = lax.psum(rel_terms, 'batch').astype(jnp.bfloat16)  142 us
    psum x1, blocking collectives, shards(): sums = lax.psum((terms[0], terms[1], terms[2]), ('feat', 'batch'))  101 us
    reduce_scatter x1, waiting for transfers between devices, shards(): lax.psum_scatter(project_every(relations, rel_weight, jnp.int32(0), own_r...  41.9 us
    another operation x1, loops' own time, aggregate(): blocks = lax.map(one_block, (sources_all, kinds_all))  41.7 us
    dot_general x16, matrix products, one_block(): parts.append(jnp.dot(tile, piece, preferred_element_type=jnp.float32))  26 us
  transfers between devices with their start and end apart: 2, of which 1 were waited for; matrix products, arithmetic and copies ran while one was open for 1% of the time, Pallas kernels for 0%

commit v1 on v0

v1 whole, which is shorter than its diff:
```python
import functools

import jax
import jax.numpy as jnp
from jax import lax
from jax.experimental import pallas as pl
from jax.experimental.pallas import tpu as pltpu
from jax.sharding import PartitionSpec as P

D = 512
HEADS = 8
HEAD_DIM = 64
NREL = 4
SLOTS = 2
SBLK = 1024
EPS = 1e-06
STEP = 128
LAG = 3
F32 = jnp.float32
BF16 = jnp.bfloat16
MESH = pl.DeviceIdType.MESH
NT = (((1,), (1,)), ((), ()))
TN = (((0,), (0,)), ((), ()))
NN = (((1,), (0,)), ((), ()))


def mm(a, b, dims=NN):
    return lax.dot_general(a, b, dims, preferred_element_type=F32)


def aggregate_kernel(src, kind, f0, f1, e0, e1, w, part, rel):
    b = pl.program_id(0)
    k0 = kind[SLOTS * b]
    k1 = kind[SLOTS * b + 1]
    p0 = mm(e0[0], f0[...])
    p1 = mm(e1[0], f1[...])
    same = k0 == k1
    first = jnp.where(same, p0 + p1, p0).astype(BF16)
    second = jnp.where(same, 0.0, p1).astype(BF16)
    rel[...] = jnp.zeros_like(rel)
    rel[k1] = second
    rel[k0] = first
    part[0, 0] = (mm(first, w[k0]) + mm(second, w[k1])).astype(BF16)


def aggregate(features, src_tile, rel_type, edge_tiles, rel_weight):
    blocks = src_tile.shape[0]
    tblk = edge_tiles.shape[1]
    cols = features.shape[1]

    def feature_block(slot):
        return pl.BlockSpec((SBLK, cols), lambda b, s, k: (s[SLOTS * b + slot], 0))

    def edge_block(slot):
        return pl.BlockSpec((1, tblk, SBLK), lambda b, s, k: (k[SLOTS * b + slot], 0, 0))

    return pl.pallas_call(
        aggregate_kernel,
        grid_spec=pltpu.PrefetchScalarGridSpec(
            num_scalar_prefetch=2,
            grid=(blocks,),
            in_specs=[
                feature_block(0),
                feature_block(1),
                edge_block(0),
                edge_block(1),
                pl.BlockSpec((NREL, cols, D), lambda b, s, k: (0, 0, 0)),
            ],
            out_specs=[
                pl.BlockSpec((1, 1, tblk, D), lambda b, s, k: (b % 2, b // 2, 0, 0)),
                pl.BlockSpec((NREL, tblk, cols), lambda b, s, k: (0, b, 0)),
            ],
        ),
        out_shape=[
            jax.ShapeDtypeStruct((2, blocks // 2, tblk, D), BF16),
            jax.ShapeDtypeStruct((NREL, blocks * tblk, cols), BF16),
        ],
        compiler_params=pltpu.CompilerParams(vmem_limit_bytes=40 * 2**20),
        name="aggregate",
    )(src_tile.reshape(-1), rel_type.reshape(-1), features, features, edge_tiles, edge_tiles, rel_weight)


def remote(src, dst, send, recv, device):
    return pltpu.make_async_remote_copy(
        src_ref=src, dst_ref=dst, send_sem=send, recv_sem=recv, device_id=device, device_id_type=MESH
    )


def step_kernel(
    nf, nb, part, rel, trow, tcol, gain, wqkv, wout, cot,
    out, grads, gain_out, grel,
    rs_sib, rs_stage, rs_recv, dt, gterm, g_sib, g_stage, g_recv,
    zl, zr, zs, gzl, gzr, gzs, gain_in, gain_z, proj, ctx, dproj,
    rs_s, rs_r, g_s, g_r, dt_s, dt_r, ag_s, ag_r, ga_s, ga_r, gz_s, gz_r,
    red_s, redl_r, redr_r, bl_s, br_s, bc_r,
):
    me = lax.axis_index("feat")
    z = lax.axis_index("batch")
    nc = nf // 2
    chip, core = me // 2, me % 2
    sib = me + 1 - 2 * core
    sibling = {"feat": sib}
    rows, cols = rel.shape[1], rel.shape[2]
    quarters = cols // STEP
    chunks = NREL * quarters
    length = out.shape[0]
    slab = D // nf

    def ahead(d):
        return 2 * ((chip + d) % nc) + core

    def behind(d):
        return 2 * ((chip + nc - d) % nc) + core

    barrier = pltpu.get_barrier_semaphore()
    pl.semaphore_signal(barrier, inc=1, device_id=sibling, device_id_type=MESH)
    for d in range(1, nc):
        pl.semaphore_signal(barrier, inc=1, device_id={"feat": ahead(d)}, device_id_type=MESH)
    for d in range(1, nb):
        pl.semaphore_signal(barrier, inc=1, device_id={"batch": (z + d) % nb}, device_id_type=MESH)
    pl.semaphore_wait(barrier, nc + nb - 1)

    def rs_pair(src, half, send, recv):
        return remote(src.at[1 - core], half, send.at[0], recv.at[0], sibling)

    def rs_chip(stage, landed, send, recv, d):
        return remote(stage.at[(chip + d) % nc], landed.at[d], send.at[d], recv.at[d], {"feat": ahead(d)})

    def rs_mid(src, half, stage, landed, send, recv):
        rs_pair(src, half, send, recv).wait_recv()
        for d in range(1, nc):
            c = (chip + d) % nc
            stage[c] = (src[core, c].astype(F32) + half[c].astype(F32)).astype(BF16)
            rs_chip(stage, landed, send, recv, d).start()

    def rs_end(src, half, stage, landed, send, recv):
        value = src[core, chip].astype(F32) + half[chip].astype(F32)
        for d in range(1, nc):
            rs_chip(stage, landed, send, recv, d).wait_recv()
            value = value + landed[d].astype(F32)
        return value

    def rs_drain(src, half, stage, landed, send, recv):
        rs_pair(src, half, send, recv).wait_send()
        for d in range(1, nc):
            rs_chip(stage, landed, send, recv, d).wait_send()

    def ag_copy(buf, send, recv, d):
        device = sibling if d == 0 else {"feat": ahead(d)}
        return remote(buf.at[me], buf.at[me], send.at[d], recv.at[d], device)

    def ag_hand(buf, send, recv, d):
        slot = behind(d)
        return remote(buf.at[slot], buf.at[slot], send.at[nc - 1 + d], recv.at[nc - 1 + d], sibling)

    def ag_landed(buf, send, recv, slot, index):
        return remote(buf.at[slot], buf.at[slot], send.at[index], recv.at[index], sibling)

    def ag_start(*group):
        for d in list(range(1, nc)) + [0]:
            ag_copy(*group, d).start()

    def ag_mid(*group):
        for d in range(1, nc):
            ag_landed(*group, behind(d), d).wait_recv()
            ag_hand(*group, d).start()

    def ag_end(*group):
        ag_landed(*group, sib, 0).wait_recv()
        for d in range(1, nc):
            ag_landed(*group, behind(d) + 1 - 2 * core, nc - 1 + d).wait_recv()

    def ag_drain(*group):
        for d in range(nc):
            ag_copy(*group, d).wait_send()
        for d in range(1, nc):
            ag_hand(*group, d).wait_send()

    total_rs = (part, rs_sib, rs_stage, rs_recv, rs_s, rs_r)
    grad_rs = (gterm, g_sib, g_stage, g_recv, g_s, g_r)
    dt_ag = (dt, dt_s, dt_r)
    grad_ag = (grads, ag_s, ag_r)
    gain_ag = (gain_in, ga_s, ga_r)

    rs_pair(part, rs_sib, rs_s, rs_r).start()
    rs_mid(*total_rs)
    total = rs_end(*total_rs)

    sigma = 1.0 / (1.0 + jnp.exp(-total))
    tokens = (total * sigma).astype(BF16).astype(F32)
    scale = lax.rsqrt(jnp.mean(tokens * tokens, axis=-1, keepdims=True) + EPS)
    normed = (tokens * scale * gain[...]).astype(BF16)
    proj[...] = mm(normed, wqkv[...]).astype(BF16)
    allowed = trow[...] <= tcol[...]
    d_ctx = mm(cot[...], wout[...], NT).astype(BF16)
    for h in range(HEADS):
        a, b = h * HEAD_DIM, (h + 1) * HEAD_DIM
        q = proj[:, a:b]
        k = proj[:, D + a : D + b]
        v = proj[:, 2 * D + a : 2 * D + b]
        scores = jnp.where(allowed, mm(q, k, NT) * (HEAD_DIM**-0.5), -1e30)
        e = jnp.exp(scores - jnp.max(scores, axis=-1, keepdims=True))
        p = e / jnp.sum(e, axis=-1, keepdims=True)
        weights = p.astype(BF16)
        ctx[:, a:b] = mm(weights, v).astype(BF16)
        dc = d_ctx[:, a:b]
        dproj[:, 2 * D + a : 2 * D + b] = mm(weights, dc, TN).astype(BF16)
        dw = mm(dc, v, NT).astype(BF16).astype(F32)
        ds = p * (dw - jnp.sum(dw * p, axis=-1, keepdims=True))
        ds = (jnp.where(allowed, ds, 0.0) * (HEAD_DIM**-0.5)).astype(BF16)
        dproj[:, a:b] = mm(ds, k).astype(BF16)
        dproj[:, D + a : D + b] = mm(ds, q, TN).astype(BF16)
    d_normed = mm(dproj[...], wqkv[...], NT).astype(BF16).astype(F32)
    u = d_normed * gain[...]
    inner = jnp.sum(u * tokens, axis=-1, keepdims=True)
    d_tokens = cot[...].astype(F32) + u * scale - tokens * (scale * scale * scale * inner * (1.0 / D))
    d_hidden = d_tokens.astype(BF16).astype(F32)
    dt[me] = (d_hidden * (sigma * (1.0 + total * (1.0 - sigma)))).astype(BF16)
    ag_start(*dt_ag)
    gain_term = jnp.sum(d_normed * (tokens * scale), axis=0, keepdims=True)
    gain_in[me] = jnp.broadcast_to(gain_term, (8, D))
    out[...] = (tokens + mm(ctx[...], wout[...])).astype(BF16)
    g_qkv = mm(normed, dproj[...], TN).astype(BF16)
    for j in range(nf):
        gterm[j % 2, j // 2, :, : 3 * D] = g_qkv[j * slab : (j + 1) * slab]
    g_out = mm(ctx[...], cot[...], TN).astype(BF16)
    for j in range(nf):
        gterm[j % 2, j // 2, :, 3 * D :] = g_out[j * slab : (j + 1) * slab]
    rs_pair(gterm, g_sib, g_s, g_r).start()
    ag_start(*gain_ag)
    ag_mid(*dt_ag)
    rs_mid(*grad_rs)
    ag_end(*dt_ag)

    owner = nb // 2 - 1 + core
    up, down = {"batch": lax.rem(z + 1, nb)}, {"batch": lax.rem(z + nb - 1, nb)}

    def hop_up(stage, landed, i):
        return remote(stage, landed, red_s.at[i], redl_r.at[i], up)

    def hop_down(stage, landed, i):
        return remote(stage, landed, red_s.at[i], redr_r.at[i], down)

    def give_up(result, i):
        return remote(result, result, br_s.at[i], bc_r.at[i], up)

    def give_down(result, i):
        return remote(result, result, bl_s.at[i], bc_r.at[i], down)

    def reduce(own, low, high, stage, result, i):
        @pl.when(z == 0)
        def _():
            stage[...] = own.astype(BF16)
            hop_up(stage, low, i).start()

        @pl.when((z > 0) & (z < owner))
        def _():
            hop_up(stage, low, i).wait_recv()
            stage[...] = (own + low[...].astype(F32)).astype(BF16)
            hop_up(stage, low, i).start()

        @pl.when(z == nb - 1)
        def _():
            stage[...] = own.astype(BF16)
            hop_down(stage, high, i).start()

        @pl.when((z > owner) & (z < nb - 1))
        def _():
            hop_down(stage, high, i).wait_recv()
            stage[...] = (own + high[...].astype(F32)).astype(BF16)
            hop_down(stage, high, i).start()

        @pl.when(z == owner)
        def _():
            hop_up(stage, low, i).wait_recv()
            hop_down(stage, high, i).wait_recv()
            result[...] = (own + low[...].astype(F32) + high[...].astype(F32)).astype(BF16)
            give_up(result, i).start()
            give_down(result, i).start()

    def spread(result, i):
        @pl.when(z != owner)
        def _():
            give_up(result, i).wait_recv()

        @pl.when((z < owner) & (z > 0))
        def _():
            give_down(result, i).start()

        @pl.when((z > owner) & (z < nb - 1))
        def _():
            give_up(result, i).start()

    def drain(low, stage, result, i):
        @pl.when(z != owner)
        def _():
            hop_up(stage, low, i).wait_send()

        @pl.when((z <= owner) & (z > 0))
        def _():
            give_down(result, i).wait_send()

        @pl.when((z >= owner) & (z < nb - 1))
        def _():
            give_up(result, i).wait_send()

    def chunk_out(i):
        return grel.at[pl.ds(pl.multiple_of(i * STEP, STEP), STEP)]

    def reduce_rel(i):
        left = rel[i // quarters, :, pl.ds(pl.multiple_of((i % quarters) * STEP, STEP), STEP)]
        own = mm(left, dt[...].reshape(rows, D), TN)
        reduce(own, zl.at[i], zr.at[i], zs.at[i], chunk_out(i), i)

    def both(i, carry):
        reduce_rel(i)
        spread(chunk_out(i - LAG), i - LAG)
        return carry

    def only_reduce(i, carry):
        reduce_rel(i)
        return carry

    def only_spread(i, carry):
        spread(chunk_out(i), i)
        return carry

    turn = max(LAG, chunks // 4)
    mine = grads.at[me]
    lax.fori_loop(0, LAG, only_reduce, 0)
    lax.fori_loop(LAG, turn, both, 0)
    ag_mid(*gain_ag)
    ag_end(*gain_ag)
    group_gain = gain_in[0]
    for j in range(1, nf):
        group_gain = group_gain + gain_in[j]
    gain_z[z] = group_gain

    def gain_copy(d):
        return remote(gain_z.at[z], gain_z.at[z], gz_s.at[d], gz_r.at[d], {"batch": (z + d) % nb})

    def gain_landed(d):
        slot = (z + nb - d) % nb
        return remote(gain_z.at[slot], gain_z.at[slot], gz_s.at[d], gz_r.at[d], {"batch": slot})

    for d in range(1, nb):
        gain_copy(d).start()
    reduce(rs_end(*grad_rs), gzl, gzr, gzs, mine, chunks)
    lax.fori_loop(turn, turn + LAG, both, 0)
    spread(mine, chunks)
    ag_start(*grad_ag)
    lax.fori_loop(turn + LAG, chunks, both, 0)
    ag_mid(*grad_ag)
    lax.fori_loop(chunks - LAG, chunks, only_spread, 0)
    for d in range(1, nb):
        gain_landed(d).wait_recv()
    whole_gain = gain_z[0]
    for j in range(1, nb):
        whole_gain = whole_gain + gain_z[j]
    gain_out[...] = whole_gain
    ag_end(*grad_ag)

    def drain_rel(i, carry):
        drain(zl.at[i], zs.at[i], chunk_out(i), i)
        return carry

    lax.fori_loop(0, chunks, drain_rel, 0)
    drain(gzl, gzs, mine, chunks)
    for d in range(1, nb):
        gain_copy(d).wait_send()
    rs_drain(*total_rs)
    rs_drain(*grad_rs)
    ag_drain(*dt_ag)
    ag_drain(*gain_ag)
    ag_drain(*grad_ag)


def training_step(nf, nb, part, rel, timestamps, gain, w_qkv, w_out, cotangent):
    nc = nf // 2
    length = timestamps.shape[0]
    cols = rel.shape[2]
    slab = D // nf
    chunks = NREL * cols // STEP
    vmem = pl.BlockSpec(memory_space=pltpu.VMEM)
    blocks = pltpu.VMEM((nc, length, D), BF16)
    slabs = pltpu.VMEM((nc, slab, 4 * D), BF16)
    pieces = pltpu.VMEM((chunks, STEP, D), BF16)
    piece = pltpu.VMEM((slab, 4 * D), BF16)
    dma = pltpu.SemaphoreType.DMA
    return pl.pallas_call(
        functools.partial(step_kernel, nf, nb),
        out_shape=[
            jax.ShapeDtypeStruct((length, D), BF16),
            jax.ShapeDtypeStruct((nf, slab, 4 * D), BF16),
            jax.ShapeDtypeStruct((8, D), F32),
            jax.ShapeDtypeStruct((NREL * cols, D), BF16),
        ],
        in_specs=[vmem] * 8,
        out_specs=[vmem] * 4,
        scratch_shapes=[
            blocks, blocks, blocks,
            pltpu.VMEM((nf, length, D), BF16),
            pltpu.VMEM((2, nc, slab, 4 * D), BF16),
            slabs, slabs, slabs,
            pieces, pieces, pieces,
            piece, piece, piece,
            pltpu.VMEM((nf, 8, D), F32),
            pltpu.VMEM((nb, 8, D), F32),
            pltpu.VMEM((length, 3 * D), BF16),
            pltpu.VMEM((length, D), BF16),
            pltpu.VMEM((length, 3 * D), BF16),
        ]
        + [dma((nc,))] * 4
        + [dma((2 * nc - 1,))] * 6
        + [dma((nb,))] * 2
        + [dma((chunks + 1,))] * 6,
        compiler_params=pltpu.CompilerParams(
            collective_id=0, has_side_effects=True, vmem_limit_bytes=52 * 2**20
        ),
        name="training_step",
    )(part, rel, timestamps.reshape(1, -1), timestamps.reshape(-1, 1), gain.reshape(1, -1), w_qkv, w_out, cotangent)


def solution(mesh):
    nf, nb = mesh.shape["feat"], mesh.shape["batch"]

    def shards(
        features, src_tile, rel_type, timestamps, edge_tiles,
        rel_weight, attn_gain, w_qkv, w_out, cotangent,
    ):
        part, rel = aggregate(features, src_tile, rel_type, edge_tiles, rel_weight)
        layer_out, grads, gain, grel = training_step(
            nf, nb, part, rel, timestamps, attn_gain, w_qkv, w_out, cotangent
        )
        grads = grads.reshape(D, 4 * D)
        return (
            layer_out,
            grads[:, : 3 * D],
            grads[:, 3 * D :],
            gain[0].astype(BF16),
            grel.reshape(NREL, rel.shape[2], D),
        )

    in_specs = (
        P("batch", "feat"),
        P("batch", None),
        P("batch", None),
        P(("batch", "feat")),
        P(),
        P(None, "feat", None),
        P(),
        P(),
        P(),
        P(("batch", "feat"), None),
    )
    out_specs = (P(("batch", "feat"), None), P(), P(), P(), P(None, "feat", None))
    return jax.shard_map(shards, mesh=mesh, in_specs=in_specs, out_specs=out_specs, check_vma=False)
```

time: 428 us -> 198 us (0.46)
  the two profiles are of different devices: /device:TPU:1 before, /device:TPU:24 now
where the time goes in v1:
time: 198 us
  Pallas kernels  183 us (92%)
  local copies, waits for them, and re-layouts  14.4 us (7%)
    pallas_call x1, Pallas kernels, training_step(): pl.pallas_call(functools.partial(step_kernel, nf, nb), out_shape=[jax.Sha...  171 us
    pallas_call x1, Pallas kernels, aggregate(): pl.pallas_call(aggregate_kernel, grid_spec=pltpu.PrefetchScalarGridSpec(n...  11.5 us
    unnamed x20, local copies, waits for them, and re-layouts  8.25 us

profile of v1, /device:TPU:24, one launch (start us, length us, event | category | flops | bytes accessed | tf_op | source)
XLA Modules:
  0.0 198.1 jit_solution(15974930126237208223)
XLA Ops:
  0.6 0.8 copy.18
  1.4 0.1 reshape.32.src
  1.5 0.8 copy.19
  2.2 0.1 reshape.33.kind
  2.3 0.8 copy.20.tcol
  3.1 0.0 copy-start.1
  3.1 1.2 copy-done.1
  4.3 0.0 copy-start.2
  4.3 1.6 copy-done.2
  5.9 0.0 copy-start.3
  5.9 11.5 %aggregate.1 = (bf16[2,4,128,512]{3,2,1,0:T(8,128)(2,1)S(1)}, bf16[4,1024,512]{2,1,0:T(8,128)(2,1)S(1)}) custom-call(s32[16]{0:T(128)S(1)} %reshape.32.src, s32[16]{0:T(128)S(1)} %reshape.33.kind, bf16[8192,512]{1,0:T(8,128)(2,1)} %f1.1, bf16[8192,512]{1,0:T(8,128)(2,1)} %f1.1, bf16[4,128,1024]{2,1,0:T(8,128)(2,1)S(1)} %copy-done.1, ...), custom_call_target="tpu_custom_call" | custom-call | tf_op jit(solution)/shard_map/aggregate/pallas_call | solution.py:57
  17.4 0.0 copy-start
  17.4 1.9 copy-done
  19.3 0.0 copy-done.3
  19.3 0.0 copy-done.4
  19.3 0.0 copy-done.5
  19.3 0.0 copy-done.6
  19.3 171.5 %training_step.1 = (bf16[128,512]{1,0:T(8,128)(2,1)S(1)}, bf16[8,64,2048]{2,1,0:T(8,128)(2,1)}, f32[8,512]{1,0:T(8,128)S(1)}, bf16[2048,512]{1,0:T(8,128)(2,1)}) custom-call(bf16[2,4,128,512]{3,2,1,0:T(8,128)(2,1)S(1)} %get-tuple-element.11.part, bf16[4,1024,512]{2,1,0:T(8,128)(2,1)} %copy-done, s32[1,128]{1,0:T(1,128)S(1)} %bitcast.7, ...), custom_call_target="tpu_custom_call" | custom-call | tf_op jit(solution)/shard_map/training_step/pallas_call | solution.py:390
  190.8 0.6 fusion
  191.4 2.0 %slice.14 = bf16[512,512]{1,0:T(8,128)(2,1)} slice(bf16[512,2048]{1,0:T(8,128)(2,1)} %bitcast.8), slice={[0:512], [1536:2048]} | slice | bytes 1048576 | tf_op jit(solution)/shard_map/slice | solution.py:439
  193.4 2.7 %slice.13 = bf16[512,1536]{1,0:T(8,128)(2,1)} slice(bf16[512,2048]{1,0:T(8,128)(2,1)} %bitcast.9), slice={[0:512], [0:1536]} | slice | bytes 3145728 | tf_op jit(solution)/shard_map/slice | solution.py:438
  196.1 0.7 copy.23
  196.7 0.0 copy-done.7
  196.7 1.3 copy.24
  (4 shorter events, 0.0 us)
Async XLA Ops:
  3.1 1.2 copy-start.1
  4.3 1.6 copy-start.2
  5.9 13.4 %copy-start.3 = (bf16[512,512]{1,0:T(8,128)(2,1)S(1)}, bf16[512,512]{1,0:T(8,128)(2,1)}, u32[]{:S(2)}) copy-start(bf16[512,512]{1,0:T(8,128)(2,1)} %wout.1) | copy-start | bytes 1572868
  5.9 13.4 %copy-start.4 = (bf16[128,512]{1,0:T(8,128)(2,1)S(1)}, bf16[128,512]{1,0:T(8,128)(2,1)}, u32[]{:S(2)}) copy-start(bf16[128,512]{1,0:T(8,128)(2,1)} %cot.1) | copy-start | bytes 393220
  5.9 13.4 %copy-start.5 = (f32[512]{0:T(512)S(1)}, f32[512]{0:T(512)}, u32[]{:S(2)}) copy-start(f32[512]{0:T(512)} %param.16) | copy-start | bytes 6148
  5.9 13.4 %copy-start.6 = (s32[128]{0:T(128)S(1)}, s32[128]{0:T(128)}, u32[]{:S(2)}) copy-start(s32[128]{0:T(128)} %param.13) | copy-start | bytes 1540
  17.4 1.9 copy-start
  191.4 5.3 %copy-start.7 = (bf16[2048,512]{1,0:T(8,128)(2,1)S(1)}, bf16[2048,512]{1,0:T(8,128)(2,1)}, u32[]{:S(2)}) copy-start(bf16[2048,512]{1,0:T(8,128)(2,1)} %get-tuple-element.16) | copy-start | bytes 6291460

commit v2 on v1

--- a/solution.py
+++ b/solution.py
@@ -15,7 +15,7 @@
 SBLK = 1024
 EPS = 1e-06
 STEP = 128
-LAG = 3
+LAG = 6
 F32 = jnp.float32
 BF16 = jnp.bfloat16
 MESH = pl.DeviceIdType.MESH
@@ -30,8 +30,8 @@
 
 def aggregate_kernel(src, kind, f0, f1, e0, e1, w, part, rel):
     b = pl.program_id(0)
-    k0 = kind[SLOTS * b]
-    k1 = kind[SLOTS * b + 1]
+    k0 = kind[0, b]
+    k1 = kind[1, b]
     p0 = mm(e0[0], f0[...])
     p1 = mm(e1[0], f1[...])
     same = k0 == k1
@@ -49,10 +49,10 @@
     cols = features.shape[1]
 
     def feature_block(slot):
-        return pl.BlockSpec((SBLK, cols), lambda b, s, k: (s[SLOTS * b + slot], 0))
+        return pl.BlockSpec((SBLK, cols), lambda b, s, k: (s[slot, b], 0))
 
     def edge_block(slot):
-        return pl.BlockSpec((1, tblk, SBLK), lambda b, s, k: (k[SLOTS * b + slot], 0, 0))
+        return pl.BlockSpec((1, tblk, SBLK), lambda b, s, k: (k[slot, b], 0, 0))
 
     return pl.pallas_call(
         aggregate_kernel,
@@ -75,9 +75,9 @@
             jax.ShapeDtypeStruct((2, blocks // 2, tblk, D), BF16),
             jax.ShapeDtypeStruct((NREL, blocks * tblk, cols), BF16),
         ],
-        compiler_params=pltpu.CompilerParams(vmem_limit_bytes=40 * 2**20),
+        compiler_params=pltpu.CompilerParams(vmem_limit_bytes=60 * 2**20),
         name="aggregate",
-    )(src_tile.reshape(-1), rel_type.reshape(-1), features, features, edge_tiles, edge_tiles, rel_weight)
+    )(src_tile.T, rel_type.T, features, features, edge_tiles, edge_tiles, rel_weight)
 
 
 def remote(src, dst, send, recv, device):
@@ -87,9 +87,9 @@
 
 
 def step_kernel(
-    nf, nb, part, rel, trow, tcol, gain, wqkv, wout, cot,
-    out, grads, gain_out, grel,
-    rs_sib, rs_stage, rs_recv, dt, gterm, g_sib, g_stage, g_recv,
+    nf, nb, part, rel, times, gain, wqkv, wout, cot,
+    out, qkv_out, w_out_out, gain_out, grel,
+    grads, rs_sib, rs_stage, rs_recv, dt, gterm, g_sib, g_stage, g_recv,
     zl, zr, zs, gzl, gzr, gzs, gain_in, gain_z, proj, ctx, dproj,
     rs_s, rs_r, g_s, g_r, dt_s, dt_r, ag_s, ag_r, ga_s, ga_r, gz_s, gz_r,
     red_s, redl_r, redr_r, bl_s, br_s, bc_r,
@@ -183,6 +183,9 @@
     gain_ag = (gain_in, ga_s, ga_r)
 
     rs_pair(part, rs_sib, rs_s, rs_r).start()
+    d_ctx = mm(cot[...], wout[...], NT).astype(BF16)
+    row_times = jnp.broadcast_to(times[...], (length, length))
+    allowed = row_times <= row_times.T
     rs_mid(*total_rs)
     total = rs_end(*total_rs)
 
@@ -191,25 +194,27 @@
     scale = lax.rsqrt(jnp.mean(tokens * tokens, axis=-1, keepdims=True) + EPS)
     normed = (tokens * scale * gain[...]).astype(BF16)
     proj[...] = mm(normed, wqkv[...]).astype(BF16)
-    allowed = trow[...] <= tcol[...]
-    d_ctx = mm(cot[...], wout[...], NT).astype(BF16)
-    for h in range(HEADS):
-        a, b = h * HEAD_DIM, (h + 1) * HEAD_DIM
-        q = proj[:, a:b]
-        k = proj[:, D + a : D + b]
-        v = proj[:, 2 * D + a : 2 * D + b]
-        scores = jnp.where(allowed, mm(q, k, NT) * (HEAD_DIM**-0.5), -1e30)
-        e = jnp.exp(scores - jnp.max(scores, axis=-1, keepdims=True))
-        p = e / jnp.sum(e, axis=-1, keepdims=True)
-        weights = p.astype(BF16)
-        ctx[:, a:b] = mm(weights, v).astype(BF16)
-        dc = d_ctx[:, a:b]
-        dproj[:, 2 * D + a : 2 * D + b] = mm(weights, dc, TN).astype(BF16)
-        dw = mm(dc, v, NT).astype(BF16).astype(F32)
-        ds = p * (dw - jnp.sum(dw * p, axis=-1, keepdims=True))
-        ds = (jnp.where(allowed, ds, 0.0) * (HEAD_DIM**-0.5)).astype(BF16)
-        dproj[:, a:b] = mm(ds, k).astype(BF16)
-        dproj[:, D + a : D + b] = mm(ds, q, TN).astype(BF16)
+    heads = range(HEADS)
+    spans = [(h * HEAD_DIM, (h + 1) * HEAD_DIM) for h in heads]
+    q = [proj[:, a:b] for a, b in spans]
+    k = [proj[:, D + a : D + b] for a, b in spans]
+    v = [proj[:, 2 * D + a : 2 * D + b] for a, b in spans]
+    dc = [d_ctx[:, a:b] for a, b in spans]
+    scores = [mm(q[h], k[h], NT) for h in heads]
+    dw = [mm(dc[h], v[h], NT) for h in heads]
+    p, ds = [], []
+    for h in heads:
+        masked = jnp.where(allowed, scores[h] * (HEAD_DIM**-0.5), -1e30)
+        e = jnp.exp(masked - jnp.max(masked, axis=-1, keepdims=True))
+        ph = e / jnp.sum(e, axis=-1, keepdims=True)
+        dwh = dw[h].astype(BF16).astype(F32)
+        dsh = ph * (dwh - jnp.sum(dwh * ph, axis=-1, keepdims=True))
+        p.append(ph.astype(BF16))
+        ds.append((jnp.where(allowed, dsh, 0.0) * (HEAD_DIM**-0.5)).astype(BF16))
+    for h, (a, b) in enumerate(spans):
+        dproj[:, a:b] = mm(ds[h], k[h]).astype(BF16)
+        dproj[:, D + a : D + b] = mm(ds[h], q[h], TN).astype(BF16)
+        dproj[:, 2 * D + a : 2 * D + b] = mm(p[h], dc[h], TN).astype(BF16)
     d_normed = mm(dproj[...], wqkv[...], NT).astype(BF16).astype(F32)
     u = d_normed * gain[...]
     inner = jnp.sum(u * tokens, axis=-1, keepdims=True)
@@ -219,6 +224,8 @@
     ag_start(*dt_ag)
     gain_term = jnp.sum(d_normed * (tokens * scale), axis=0, keepdims=True)
     gain_in[me] = jnp.broadcast_to(gain_term, (8, D))
+    for h, (a, b) in enumerate(spans):
+        ctx[:, a:b] = mm(p[h], v[h]).astype(BF16)
     out[...] = (tokens + mm(ctx[...], wout[...])).astype(BF16)
     g_qkv = mm(normed, dproj[...], TN).astype(BF16)
     for j in range(nf):
@@ -278,18 +285,23 @@
             give_up(result, i).start()
             give_down(result, i).start()
 
+    edge = (z == 0) | (z == nb - 1)
+
     def spread(result, i):
-        @pl.when(z != owner)
+        @pl.when((z > 0) & (z < owner))
+        def _():
+            give_down(result, i).wait_recv()
+            give_down(result, i).start()
+
+        @pl.when((z > owner) & (z < nb - 1))
         def _():
             give_up(result, i).wait_recv()
-
-        @pl.when((z < owner) & (z > 0))
-        def _():
-            give_down(result, i).start()
-
-        @pl.when((z > owner) & (z < nb - 1))
-        def _():
             give_up(result, i).start()
+
+    def settle(result, i):
+        @pl.when(edge)
+        def _():
+            give_up(result, i).wait_recv()
 
     def drain(low, stage, result, i):
         @pl.when(z != owner)
@@ -314,7 +326,7 @@
 
     def both(i, carry):
         reduce_rel(i)
-        spread(chunk_out(i - LAG), i - LAG)
+        spread(chunk_out(i - lag), i - lag)
         return carry
 
     def only_reduce(i, carry):
@@ -325,10 +337,14 @@
         spread(chunk_out(i), i)
         return carry
 
-    turn = max(LAG, chunks // 4)
+    def only_settle(i, carry):
+        settle(chunk_out(i), i)
+        return carry
+
+    lag = min(LAG, chunks // 2)
+    turn = lag
     mine = grads.at[me]
-    lax.fori_loop(0, LAG, only_reduce, 0)
-    lax.fori_loop(LAG, turn, both, 0)
+    lax.fori_loop(0, lag, only_reduce, 0)
     ag_mid(*gain_ag)
     ag_end(*gain_ag)
     group_gain = gain_in[0]
@@ -346,12 +362,23 @@
     for d in range(1, nb):
         gain_copy(d).start()
     reduce(rs_end(*grad_rs), gzl, gzr, gzs, mine, chunks)
-    lax.fori_loop(turn, turn + LAG, both, 0)
+    lax.fori_loop(turn, turn + lag, both, 0)
     spread(mine, chunks)
-    ag_start(*grad_ag)
-    lax.fori_loop(turn + LAG, chunks, both, 0)
+
+    @pl.when(jnp.logical_not(edge))
+    def _():
+        ag_start(*grad_ag)
+
+    lax.fori_loop(turn + lag, chunks, both, 0)
+    settle(mine, chunks)
+
+    @pl.when(edge)
+    def _():
+        ag_start(*grad_ag)
+
     ag_mid(*grad_ag)
-    lax.fori_loop(chunks - LAG, chunks, only_spread, 0)
+    lax.fori_loop(chunks - lag, chunks, only_spread, 0)
+    lax.fori_loop(0, chunks, only_settle, 0)
     for d in range(1, nb):
         gain_landed(d).wait_recv()
     whole_gain = gain_z[0]
@@ -359,6 +386,9 @@
         whole_gain = whole_gain + gain_z[j]
     gain_out[...] = whole_gain
     ag_end(*grad_ag)
+    for j in range(nf):
+        qkv_out[j * slab : (j + 1) * slab] = grads[j, :, : 3 * D]
+        w_out_out[j * slab : (j + 1) * slab] = grads[j, :, 3 * D :]
 
     def drain_rel(i, carry):
         drain(zl.at[i], zs.at[i], chunk_out(i), i)
@@ -391,13 +421,15 @@
         functools.partial(step_kernel, nf, nb),
         out_shape=[
             jax.ShapeDtypeStruct((length, D), BF16),
-            jax.ShapeDtypeStruct((nf, slab, 4 * D), BF16),
+            jax.ShapeDtypeStruct((D, 3 * D), BF16),
+            jax.ShapeDtypeStruct((D, D), BF16),
             jax.ShapeDtypeStruct((8, D), F32),
             jax.ShapeDtypeStruct((NREL * cols, D), BF16),
         ],
-        in_specs=[vmem] * 8,
-        out_specs=[vmem] * 4,
+        in_specs=[vmem] * 7,
+        out_specs=[vmem] * 5,
         scratch_shapes=[
+            pltpu.VMEM((nf, slab, 4 * D), BF16),
             blocks, blocks, blocks,
             pltpu.VMEM((nf, length, D), BF16),
             pltpu.VMEM((2, nc, slab, 4 * D), BF16),
@@ -415,10 +447,10 @@
         + [dma((nb,))] * 2
         + [dma((chunks + 1,))] * 6,
         compiler_params=pltpu.CompilerParams(
-            collective_id=0, has_side_effects=True, vmem_limit_bytes=52 * 2**20
+            collective_id=0, has_side_effects=True, vmem_limit_bytes=60 * 2**20
         ),
         name="training_step",
-    )(part, rel, timestamps.reshape(1, -1), timestamps.reshape(-1, 1), gain.reshape(1, -1), w_qkv, w_out, cotangent)
+    )(part, rel, timestamps.reshape(1, -1), gain.reshape(1, -1), w_qkv, w_out, cotangent)
 
 
 def solution(mesh):
@@ -429,14 +461,13 @@
         rel_weight, attn_gain, w_qkv, w_out, cotangent,
     ):
         part, rel = aggregate(features, src_tile, rel_type, edge_tiles, rel_weight)
-        layer_out, grads, gain, grel = training_step(
+        layer_out, grad_qkv, grad_out, gain, grel = training_step(
             nf, nb, part, rel, timestamps, attn_gain, w_qkv, w_out, cotangent
         )
-        grads = grads.reshape(D, 4 * D)
         return (
             layer_out,
-            grads[:, : 3 * D],
-            grads[:, 3 * D :],
+            grad_qkv,
+            grad_out,
             gain[0].astype(BF16),
             grel.reshape(NREL, rel.shape[2], D),
         )

time: 198 us -> 130 us (0.66)
  the two profiles are of different devices: /device:TPU:24 before, /device:TPU:1 now
where the time goes in v2:
time: 130 us
  Pallas kernels  121 us (93%)
  local copies, waits for them, and re-layouts  7.84 us (6%)
    pallas_call x1, Pallas kernels, training_step(): pl.pallas_call(functools.partial(step_kernel, nf, nb), out_shape=[jax.Sha...  107 us
    pallas_call x1, Pallas kernels, aggregate(): pl.pallas_call(aggregate_kernel, grid_spec=pltpu.PrefetchScalarGridSpec(n...  14.4 us
    unnamed x8, local copies, waits for them, and re-layouts  6.49 us

profile of v2, /device:TPU:1, one launch (start us, length us, event | category | flops | bytes accessed | tf_op | source)
XLA Modules:
  0.0 129.8 jit_solution(1113088201826518482)
XLA Ops:
  0.6 14.4 %aggregate.1 = (bf16[2,4,128,512]{3,2,1,0:T(8,128)(2,1)}, bf16[4,1024,512]{2,1,0:T(8,128)(2,1)}) custom-call(s32[2,8]{1,0:T(2,128)} %bitcast.7, s32[2,8]{1,0:T(2,128)} %bitcast.8, bf16[8192,512]{1,0:T(8,128)(2,1)} %f1.1, bf16[8192,512]{1,0:T(8,128)(2,1)} %f1.1, bf16[4,128,1024]{2,1,0:T(8,128)(2,1)} %e1.1, bf16[4,128,1024]{2,1,0:T(8,128)(2,1)} %e1.1, ...), custom_call_target="tpu_custom_call" | custom-call | tf_op jit(solution)/shard_map/aggregate/pallas_call | solution.py:57
  15.0 107.0 %training_step.1 = (bf16[128,512]{1,0:T(8,128)(2,1)}, bf16[512,1536]{1,0:T(8,128)(2,1)}, bf16[512,512]{1,0:T(8,128)(2,1)}, f32[8,512]{1,0:T(8,128)}, bf16[2048,512]{1,0:T(8,128)(2,1)}) custom-call(bf16[2,4,128,512]{3,2,1,0:T(8,128)(2,1)} %get-tuple-element.12.part, bf16[4,1024,512]{2,1,0:T(8,128)(2,1)} %get-tuple-element.13.rel, s32[1,128]{1,0:T(1,128)} %bitcast.9, ...), custom_call_target="tpu_custom_call" | custom-call | tf_op jit(solution)/shard_map/training_step/pallas_call | solution.py:420
  122.0 0.0 copy-start.1
  122.0 1.4 %fusion = bf16[512]{0:T(512)(128)(2,1)} fusion(f32[8,512]{1,0:T(8,128)} %get-tuple-element.17), kind=kLoop, calls=%fused_computation.1 | loop fusion | bytes 2048 | tf_op jit(solution)/shard_map/slice | solution.py:471
  123.3 1.6 %copy.19 = bf16[128,512]{1,0:T(8,128)(2,1)} copy(bf16[128,512]{1,0:T(8,128)(2,1)} %get-tuple-element.24) | data formatting | bytes 262144
  124.9 0.0 copy-start
  124.9 2.8 %copy.20 = bf16[512,1536]{1,0:T(8,128)(2,1)} copy(bf16[512,1536]{1,0:T(8,128)(2,1)} %get-tuple-element.25) | data formatting | bytes 3145728
  127.7 0.0 copy-done.1
  127.7 0.8 copy.21
  128.5 0.0 copy-done
  128.5 1.3 %copy.22 = bf16[4,512,512]{2,1,0:T(8,128)(2,1)} copy(bf16[4,512,512]{2,1,0:T(8,128)(2,1)S(1)} %bitcast.5) | data formatting | bytes 4194304
Async XLA Ops:
  122.0 5.7 %copy-start.1 = (bf16[512,512]{1,0:T(8,128)(2,1)S(1)}, bf16[512,512]{1,0:T(8,128)(2,1)}, u32[]{:S(2)}) copy-start(bf16[512,512]{1,0:T(8,128)(2,1)} %get-tuple-element.26) | copy-start | bytes 1572868
  124.9 3.6 %copy-start = (bf16[2048,512]{1,0:T(8,128)(2,1)S(1)}, bf16[2048,512]{1,0:T(8,128)(2,1)}, u32[]{:S(2)}) copy-start(bf16[2048,512]{1,0:T(8,128)(2,1)} %get-tuple-element.18) | copy-start | bytes 6291460

commit v3 on v2

--- a/solution.py
+++ b/solution.py
@@ -28,58 +28,6 @@
     return lax.dot_general(a, b, dims, preferred_element_type=F32)
 
 
-def aggregate_kernel(src, kind, f0, f1, e0, e1, w, part, rel):
-    b = pl.program_id(0)
-    k0 = kind[0, b]
-    k1 = kind[1, b]
-    p0 = mm(e0[0], f0[...])
-    p1 = mm(e1[0], f1[...])
-    same = k0 == k1
-    first = jnp.where(same, p0 + p1, p0).astype(BF16)
-    second = jnp.where(same, 0.0, p1).astype(BF16)
-    rel[...] = jnp.zeros_like(rel)
-    rel[k1] = second
-    rel[k0] = first
-    part[0, 0] = (mm(first, w[k0]) + mm(second, w[k1])).astype(BF16)
-
-
-def aggregate(features, src_tile, rel_type, edge_tiles, rel_weight):
-    blocks = src_tile.shape[0]
-    tblk = edge_tiles.shape[1]
-    cols = features.shape[1]
-
-    def feature_block(slot):
-        return pl.BlockSpec((SBLK, cols), lambda b, s, k: (s[slot, b], 0))
-
-    def edge_block(slot):
-        return pl.BlockSpec((1, tblk, SBLK), lambda b, s, k: (k[slot, b], 0, 0))
-
-    return pl.pallas_call(
-        aggregate_kernel,
-        grid_spec=pltpu.PrefetchScalarGridSpec(
-            num_scalar_prefetch=2,
-            grid=(blocks,),
-            in_specs=[
-                feature_block(0),
-                feature_block(1),
-                edge_block(0),
-                edge_block(1),
-                pl.BlockSpec((NREL, cols, D), lambda b, s, k: (0, 0, 0)),
-            ],
-            out_specs=[
-                pl.BlockSpec((1, 1, tblk, D), lambda b, s, k: (b % 2, b // 2, 0, 0)),
-                pl.BlockSpec((NREL, tblk, cols), lambda b, s, k: (0, b, 0)),
-            ],
-        ),
-        out_shape=[
-            jax.ShapeDtypeStruct((2, blocks // 2, tblk, D), BF16),
-            jax.ShapeDtypeStruct((NREL, blocks * tblk, cols), BF16),
-        ],
-        compiler_params=pltpu.CompilerParams(vmem_limit_bytes=60 * 2**20),
-        name="aggregate",
-    )(src_tile.T, rel_type.T, features, features, edge_tiles, edge_tiles, rel_weight)
-
-
 def remote(src, dst, send, recv, device):
     return pltpu.make_async_remote_copy(
         src_ref=src, dst_ref=dst, send_sem=send, recv_sem=recv, device_id=device, device_id_type=MESH
@@ -87,9 +35,9 @@
 
 
 def step_kernel(
-    nf, nb, part, rel, times, gain, wqkv, wout, cot,
+    nf, nb, features, src, kind, edges, rel_w, times, gain, wqkv, wout, cot,
     out, qkv_out, w_out_out, gain_out, grel,
-    grads, rs_sib, rs_stage, rs_recv, dt, gterm, g_sib, g_stage, g_recv,
+    feats, feats_sem, part, rel, grads, rs_sib, rs_stage, rs_recv, dt, gterm, g_sib, g_stage, g_recv,
     zl, zr, zs, gzl, gzr, gzs, gain_in, gain_z, proj, ctx, dproj,
     rs_s, rs_r, g_s, g_r, dt_s, dt_r, ag_s, ag_r, ga_s, ga_r, gz_s, gz_r,
     red_s, redl_r, redr_r, bl_s, br_s, bc_r,
@@ -101,9 +49,9 @@
     sib = me + 1 - 2 * core
     sibling = {"feat": sib}
     rows, cols = rel.shape[1], rel.shape[2]
+    length = out.shape[0]
     quarters = cols // STEP
     chunks = NREL * quarters
-    length = out.shape[0]
     slab = D // nf
 
     def ahead(d):
@@ -112,6 +60,8 @@
     def behind(d):
         return 2 * ((chip + nc - d) % nc) + core
 
+    feats_copy = pltpu.make_async_copy(features, feats, feats_sem)
+    feats_copy.start()
     barrier = pltpu.get_barrier_semaphore()
     pl.semaphore_signal(barrier, inc=1, device_id=sibling, device_id_type=MESH)
     for d in range(1, nc):
@@ -176,18 +126,57 @@
         for d in range(1, nc):
             ag_hand(*group, d).wait_send()
 
-    total_rs = (part, rs_sib, rs_stage, rs_recv, rs_s, rs_r)
     grad_rs = (gterm, g_sib, g_stage, g_recv, g_s, g_r)
     dt_ag = (dt, dt_s, dt_r)
     grad_ag = (grads, ag_s, ag_r)
     gain_ag = (gain_in, ga_s, ga_r)
 
-    rs_pair(part, rs_sib, rs_s, rs_r).start()
+    def project(half, c):
+        b = 2 * c + half
+        k0, k1 = kind[0, b], kind[1, b]
+        p0 = mm(edges[k0], feats[src[0, b]])
+        p1 = mm(edges[k1], feats[src[1, b]])
+        same = (k0 == k1).astype(F32)
+        first = (p0 + same * p1).astype(BF16)
+        second = ((1.0 - same) * p1).astype(BF16)
+        here = pl.ds(pl.multiple_of(b * length, length), length)
+        for relation in range(NREL):
+            is_first = (k0 == relation).astype(F32)
+            is_second = (k1 == relation).astype(F32)
+            rel[relation, here, :] = (is_first * first.astype(F32) + is_second * second.astype(F32)).astype(BF16)
+        part[half, c] = (mm(first, rel_w[k0]) + mm(second, rel_w[k1])).astype(BF16)
+
+    def to_sibling(c):
+        return remote(part.at[1 - core, c], rs_sib.at[c], rs_s.at[nc + c], rs_r.at[nc + c], sibling)
+
+    def to_chip(d):
+        return rs_chip(rs_stage, rs_recv, rs_s, rs_r, d)
+
+    def other_half(c, carry):
+        project(1 - core, c)
+        to_sibling(c).start()
+        return carry
+
+    def own_half(d, carry):
+        c = (chip + d) % nc
+        project(core, c)
+        to_sibling(c).wait_recv()
+        rs_stage[c] = (part[core, c].astype(F32) + rs_sib[c].astype(F32)).astype(BF16)
+        to_chip(d).start()
+        return carry
+
+    feats_copy.wait()
+    lax.fori_loop(0, nc, other_half, 0)
+    lax.fori_loop(1, nc, own_half, 0)
+    project(core, chip)
     d_ctx = mm(cot[...], wout[...], NT).astype(BF16)
     row_times = jnp.broadcast_to(times[...], (length, length))
     allowed = row_times <= row_times.T
-    rs_mid(*total_rs)
-    total = rs_end(*total_rs)
+    to_sibling(chip).wait_recv()
+    total = part[core, chip].astype(F32) + rs_sib[chip].astype(F32)
+    for d in range(1, nc):
+        to_chip(d).wait_recv()
+        total = total + rs_recv[d].astype(F32)
 
     sigma = 1.0 / (1.0 + jnp.exp(-total))
     tokens = (total * sigma).astype(BF16).astype(F32)
@@ -398,17 +387,22 @@
     drain(gzl, gzs, mine, chunks)
     for d in range(1, nb):
         gain_copy(d).wait_send()
-    rs_drain(*total_rs)
+    for c in range(nc):
+        to_sibling(c).wait_send()
+    for d in range(1, nc):
+        to_chip(d).wait_send()
     rs_drain(*grad_rs)
     ag_drain(*dt_ag)
     ag_drain(*gain_ag)
     ag_drain(*grad_ag)
 
 
-def training_step(nf, nb, part, rel, timestamps, gain, w_qkv, w_out, cotangent):
+def training_step(
+    nf, nb, features, src_tile, rel_type, edge_tiles, rel_weight, timestamps, gain, w_qkv, w_out, cotangent
+):
     nc = nf // 2
     length = timestamps.shape[0]
-    cols = rel.shape[2]
+    cols = features.shape[1]
     slab = D // nf
     chunks = NREL * cols // STEP
     vmem = pl.BlockSpec(memory_space=pltpu.VMEM)
@@ -426,9 +420,15 @@
             jax.ShapeDtypeStruct((8, D), F32),
             jax.ShapeDtypeStruct((NREL * cols, D), BF16),
         ],
-        in_specs=[vmem] * 7,
+        in_specs=[pl.BlockSpec(memory_space=pl.ANY)]
+        + [pl.BlockSpec(memory_space=pltpu.SMEM)] * 2
+        + [vmem] * 7,
         out_specs=[vmem] * 5,
         scratch_shapes=[
+            pltpu.VMEM((features.shape[0] // SBLK, SBLK, cols), BF16),
+            dma(()),
+            pltpu.VMEM((2, nc, length, D), BF16),
+            pltpu.VMEM((NREL, nf * length, cols), BF16),
             pltpu.VMEM((nf, slab, 4 * D), BF16),
             blocks, blocks, blocks,
             pltpu.VMEM((nf, length, D), BF16),
@@ -442,7 +442,8 @@
             pltpu.VMEM((length, D), BF16),
             pltpu.VMEM((length, 3 * D), BF16),
         ]
-        + [dma((nc,))] * 4
+        + [dma((2 * nc,))] * 2
+        + [dma((nc,))] * 2
         + [dma((2 * nc - 1,))] * 6
         + [dma((nb,))] * 2
         + [dma((chunks + 1,))] * 6,
@@ -450,7 +451,43 @@
             collective_id=0, has_side_effects=True, vmem_limit_bytes=60 * 2**20
         ),
         name="training_step",
-    )(part, rel, timestamps.reshape(1, -1), gain.reshape(1, -1), w_qkv, w_out, cotangent)
+    )(
+        features.reshape(-1, SBLK, cols), src_tile.T, rel_type.T, edge_tiles, rel_weight,
+        timestamps.reshape(1, -1), gain.reshape(1, -1), w_qkv, w_out, cotangent,
+    )
+
+
+def hand_out_kernel(count, *refs):
+    arrays, gain = refs[:count], refs[count]
+    results, gain_out, sems = refs[count + 1 : -2], refs[-2], refs[-1]
+    copies = []
+    for array, result in zip(arrays, results):
+        piece = min(512, array.shape[0])
+        for start in range(0, array.shape[0], piece):
+            span = pl.ds(start, piece)
+            copies.append((array.at[span], result.at[span]))
+    copies = [pltpu.make_async_copy(a, b, sems.at[i]) for i, (a, b) in enumerate(copies)]
+    for copy in copies:
+        copy.start()
+    gain_out[...] = gain[0].astype(BF16)
+    for copy in copies:
+        copy.wait()
+
+
+def hand_out(arrays, gain):
+    anywhere = pl.BlockSpec(memory_space=pl.ANY)
+    vmem = pl.BlockSpec(memory_space=pltpu.VMEM)
+    pieces = sum(max(1, array.shape[0] // 512) for array in arrays)
+    return pl.pallas_call(
+        functools.partial(hand_out_kernel, len(arrays)),
+        out_shape=[jax.ShapeDtypeStruct(a.shape, a.dtype) for a in arrays]
+        + [jax.ShapeDtypeStruct((D,), BF16)],
+        in_specs=[anywhere] * len(arrays) + [vmem],
+        out_specs=[anywhere] * len(arrays) + [vmem],
+        scratch_shapes=[pltpu.SemaphoreType.DMA((pieces,))],
+        compiler_params=pltpu.CompilerParams(vmem_limit_bytes=60 * 2**20),
+        name="hand_out",
+    )(*arrays, gain)
 
 
 def solution(mesh):
@@ -460,17 +497,12 @@
         features, src_tile, rel_type, timestamps, edge_tiles,
         rel_weight, attn_gain, w_qkv, w_out, cotangent,
     ):
-        part, rel = aggregate(features, src_tile, rel_type, edge_tiles, rel_weight)
-        layer_out, grad_qkv, grad_out, gain, grel = training_step(
-            nf, nb, part, rel, timestamps, attn_gain, w_qkv, w_out, cotangent
+        *results, gain, grel = training_step(
+            nf, nb, features, src_tile, rel_type, edge_tiles, rel_weight,
+            timestamps, attn_gain, w_qkv, w_out, cotangent,
         )
-        return (
-            layer_out,
-            grad_qkv,
-            grad_out,
-            gain[0].astype(BF16),
-            grel.reshape(NREL, rel.shape[2], D),
-        )
+        layer_out, grad_qkv, grad_out, grel, gain = hand_out((*results, grel), gain)
+        return layer_out, grad_qkv, grad_out, gain, grel.reshape(NREL, features.shape[1], D)
 
     in_specs = (
         P("batch", "feat"),

time: 130 us -> 244 us (1.88)
  Pallas kernels: 121 us -> 243 us
  local copies, waits for them, and re-layouts: 7.84 us -> 0 us
    pallas_call x1, Pallas kernels: 14.4 us -> 133 us  [hand_out(): pl.pallas_call(functools.partial(hand_out_kernel, len(arrays)), out_shape...]
    unnamed x8 -> x0, local copies, waits for them, and re-layouts: 6.49 us -> none
    pallas_call x1, Pallas kernels: 107 us -> 110 us  [training_step(): pl.pallas_call(functools.partial(step_kernel, nf, nb), out_shape=[jax.Sha...]
where the time goes in v3:
time: 244 us
  Pallas kernels  243 us (100%)
    pallas_call x1, Pallas kernels, hand_out(): pl.pallas_call(functools.partial(hand_out_kernel, len(arrays)), out_shape...  133 us
    pallas_call x1, Pallas kernels, training_step(): pl.pallas_call(functools.partial(step_kernel, nf, nb), out_shape=[jax.Sha...  110 us

profile of v3, /device:TPU:1, one launch (start us, length us, event | category | flops | bytes accessed | tf_op | source)
XLA Modules:
  0.0 243.9 jit_solution(4957986724260601878)
XLA Ops:
  0.6 109.8 %training_step.1 = (bf16[128,512]{1,0:T(8,128)(2,1)}, bf16[512,1536]{1,0:T(8,128)(2,1)}, bf16[512,512]{1,0:T(8,128)(2,1)}, f32[8,512]{1,0:T(8,128)}, bf16[2048,512]{1,0:T(8,128)(2,1)}) custom-call(bf16[8,1024,512]{2,1,0:T(8,128)(2,1)} %bitcast.6, s32[2,8]{1,0:T(2,128)} %bitcast.8, s32[2,8]{1,0:T(2,128)} %bitcast.9, bf16[4,128,1024]{2,1,0:T(8,128)(2,1)} %edges.1, ...), custom_call_target="tpu_custom_call" | custom-call | tf_op jit(solution)/shard_map/training_step/pallas_call | solution.py:414
  110.4 133.5 %hand_out.1 = (bf16[128,512]{1,0:T(8,128)(2,1)}, bf16[512,1536]{1,0:T(8,128)(2,1)}, bf16[512,512]{1,0:T(8,128)(2,1)}, bf16[2048,512]{1,0:T(8,128)(2,1)}, bf16[512]{0:T(512)(128)(2,1)}) custom-call(bf16[128,512]{1,0:T(8,128)(2,1)} %get-tuple-element.15.refs_0_, bf16[512,1536]{1,0:T(8,128)(2,1)} %get-tuple-element.16.refs_1_, ...), custom_call_target="tpu_custom_call" | custom-call | tf_op jit(solution)/shard_map/hand_out/pallas_call | solution.py:481

commit v4 on v3

--- a/solution.py
+++ b/solution.py
@@ -16,6 +16,7 @@
 EPS = 1e-06
 STEP = 128
 LAG = 6
+PIECE = 64
 F32 = jnp.float32
 BF16 = jnp.bfloat16
 MESH = pl.DeviceIdType.MESH
@@ -53,6 +54,9 @@
     quarters = cols // STEP
     chunks = NREL * quarters
     slab = D // nf
+    split = STEP // PIECE
+    pieces = split * chunks
+    lag = min(LAG, chunks // 2)
 
     def ahead(d):
         return 2 * ((chip + d) % nc) + core
@@ -306,20 +310,24 @@
             give_up(result, i).wait_send()
 
     def chunk_out(i):
-        return grel.at[pl.ds(pl.multiple_of(i * STEP, STEP), STEP)]
-
-    def reduce_rel(i):
+        return grel.at[pl.ds(pl.multiple_of(i * PIECE, PIECE), PIECE)]
+
+    def reduce_rel(i, behind_too):
         left = rel[i // quarters, :, pl.ds(pl.multiple_of((i % quarters) * STEP, STEP), STEP)]
         own = mm(left, dt[...].reshape(rows, D), TN)
-        reduce(own, zl.at[i], zr.at[i], zs.at[i], chunk_out(i), i)
+        for half in range(split):
+            j = split * i + half
+            mine_now = own[half * PIECE : (half + 1) * PIECE]
+            reduce(mine_now, zl.at[j], zr.at[j], zs.at[j], chunk_out(j), j)
+            if behind_too:
+                spread(chunk_out(j - split * lag), j - split * lag)
 
     def both(i, carry):
-        reduce_rel(i)
-        spread(chunk_out(i - lag), i - lag)
+        reduce_rel(i, True)
         return carry
 
     def only_reduce(i, carry):
-        reduce_rel(i)
+        reduce_rel(i, False)
         return carry
 
     def only_spread(i, carry):
@@ -330,7 +338,6 @@
         settle(chunk_out(i), i)
         return carry
 
-    lag = min(LAG, chunks // 2)
     turn = lag
     mine = grads.at[me]
     lax.fori_loop(0, lag, only_reduce, 0)
@@ -350,24 +357,23 @@
 
     for d in range(1, nb):
         gain_copy(d).start()
-    reduce(rs_end(*grad_rs), gzl, gzr, gzs, mine, chunks)
+    reduce(rs_end(*grad_rs), gzl, gzr, gzs, mine, pieces)
     lax.fori_loop(turn, turn + lag, both, 0)
-    spread(mine, chunks)
+    spread(mine, pieces)
 
     @pl.when(jnp.logical_not(edge))
     def _():
         ag_start(*grad_ag)
 
     lax.fori_loop(turn + lag, chunks, both, 0)
-    settle(mine, chunks)
+    settle(mine, pieces)
 
     @pl.when(edge)
     def _():
         ag_start(*grad_ag)
 
+    lax.fori_loop(pieces - split * lag, pieces, only_spread, 0)
     ag_mid(*grad_ag)
-    lax.fori_loop(chunks - lag, chunks, only_spread, 0)
-    lax.fori_loop(0, chunks, only_settle, 0)
     for d in range(1, nb):
         gain_landed(d).wait_recv()
     whole_gain = gain_z[0]
@@ -378,13 +384,14 @@
     for j in range(nf):
         qkv_out[j * slab : (j + 1) * slab] = grads[j, :, : 3 * D]
         w_out_out[j * slab : (j + 1) * slab] = grads[j, :, 3 * D :]
+    lax.fori_loop(0, pieces, only_settle, 0)
 
     def drain_rel(i, carry):
         drain(zl.at[i], zs.at[i], chunk_out(i), i)
         return carry
 
-    lax.fori_loop(0, chunks, drain_rel, 0)
-    drain(gzl, gzs, mine, chunks)
+    lax.fori_loop(0, pieces, drain_rel, 0)
+    drain(gzl, gzs, mine, pieces)
     for d in range(1, nb):
         gain_copy(d).wait_send()
     for c in range(nc):
@@ -404,11 +411,11 @@
     length = timestamps.shape[0]
     cols = features.shape[1]
     slab = D // nf
-    chunks = NREL * cols // STEP
+    pieces = NREL * cols // PIECE
     vmem = pl.BlockSpec(memory_space=pltpu.VMEM)
     blocks = pltpu.VMEM((nc, length, D), BF16)
     slabs = pltpu.VMEM((nc, slab, 4 * D), BF16)
-    pieces = pltpu.VMEM((chunks, STEP, D), BF16)
+    lines = pltpu.VMEM((pieces, PIECE, D), BF16)
     piece = pltpu.VMEM((slab, 4 * D), BF16)
     dma = pltpu.SemaphoreType.DMA
     return pl.pallas_call(
@@ -434,7 +441,7 @@
             pltpu.VMEM((nf, length, D), BF16),
             pltpu.VMEM((2, nc, slab, 4 * D), BF16),
             slabs, slabs, slabs,
-            pieces, pieces, pieces,
+            lines, lines, lines,
             piece, piece, piece,
             pltpu.VMEM((nf, 8, D), F32),
             pltpu.VMEM((nb, 8, D), F32),
@@ -446,7 +453,7 @@
         + [dma((nc,))] * 2
         + [dma((2 * nc - 1,))] * 6
         + [dma((nb,))] * 2
-        + [dma((chunks + 1,))] * 6,
+        + [dma((pieces + 1,))] * 6,
         compiler_params=pltpu.CompilerParams(
             collective_id=0, has_side_effects=True, vmem_limit_bytes=60 * 2**20
         ),
@@ -457,34 +464,23 @@
     )
 
 
-def hand_out_kernel(count, *refs):
-    arrays, gain = refs[:count], refs[count]
-    results, gain_out, sems = refs[count + 1 : -2], refs[-2], refs[-1]
-    copies = []
-    for array, result in zip(arrays, results):
-        piece = min(512, array.shape[0])
-        for start in range(0, array.shape[0], piece):
-            span = pl.ds(start, piece)
-            copies.append((array.at[span], result.at[span]))
-    copies = [pltpu.make_async_copy(a, b, sems.at[i]) for i, (a, b) in enumerate(copies)]
-    for copy in copies:
-        copy.start()
-    gain_out[...] = gain[0].astype(BF16)
-    for copy in copies:
-        copy.wait()
+def hand_out_kernel(*refs):
+    half = len(refs) // 2
+    for array, result in zip(refs[: half - 1], refs[half:-1]):
+        result[...] = array[...]
+    refs[-1][...] = refs[half - 1][0].astype(BF16)
 
 
 def hand_out(arrays, gain):
-    anywhere = pl.BlockSpec(memory_space=pl.ANY)
-    vmem = pl.BlockSpec(memory_space=pltpu.VMEM)
-    pieces = sum(max(1, array.shape[0] // 512) for array in arrays)
+    steps = 4
+    specs = [pl.BlockSpec((a.shape[0] // steps, a.shape[1]), lambda i: (i, 0)) for a in arrays]
     return pl.pallas_call(
-        functools.partial(hand_out_kernel, len(arrays)),
+        hand_out_kernel,
+        grid=(steps,),
         out_shape=[jax.ShapeDtypeStruct(a.shape, a.dtype) for a in arrays]
         + [jax.ShapeDtypeStruct((D,), BF16)],
-        in_specs=[anywhere] * len(arrays) + [vmem],
-        out_specs=[anywhere] * len(arrays) + [vmem],
-        scratch_shapes=[pltpu.SemaphoreType.DMA((pieces,))],
+        in_specs=specs + [pl.BlockSpec(gain.shape, lambda i: (0, 0))],
+        out_specs=specs + [pl.BlockSpec((D,), lambda i: (0,))],
         compiler_params=pltpu.CompilerParams(vmem_limit_bytes=60 * 2**20),
         name="hand_out",
     )(*arrays, gain)

time: 244 us -> 116 us (0.48)
  Pallas kernels: 243 us -> 115 us
    pallas_call x1, Pallas kernels: 133 us -> 4.81 us  [hand_out(): pl.pallas_call(hand_out_kernel, grid=(steps,), out_shape=[jax.ShapeDtypeS...]
where the time goes in v4:
time: 116 us
  Pallas kernels  115 us (99%)
    pallas_call x1, Pallas kernels, training_step(): pl.pallas_call(functools.partial(step_kernel, nf, nb), out_shape=[jax.Sha...  110 us
    pallas_call x1, Pallas kernels, hand_out(): pl.pallas_call(hand_out_kernel, grid=(steps,), out_shape=[jax.ShapeDtypeS...  4.81 us

profile of v4, /device:TPU:1, one launch (start us, length us, event | category | flops | bytes accessed | tf_op | source)
XLA Modules:
  0.0 115.6 jit_solution(384541532323508409)
XLA Ops:
  0.6 110.2 %training_step.1 = (bf16[128,512]{1,0:T(8,128)(2,1)}, bf16[512,1536]{1,0:T(8,128)(2,1)}, bf16[512,512]{1,0:T(8,128)(2,1)}, f32[8,512]{1,0:T(8,128)}, bf16[2048,512]{1,0:T(8,128)(2,1)}) custom-call(bf16[8,1024,512]{2,1,0:T(8,128)(2,1)} %bitcast.6, s32[2,8]{1,0:T(2,128)} %bitcast.8, s32[2,8]{1,0:T(2,128)} %bitcast.9, bf16[4,128,1024]{2,1,0:T(8,128)(2,1)} %edges.1, ...), custom_call_target="tpu_custom_call" | custom-call | tf_op jit(solution)/shard_map/training_step/pallas_call | solution.py:421
  110.8 4.8 %hand_out.1 = (bf16[128,512]{1,0:T(8,128)(2,1)}, bf16[512,1536]{1,0:T(8,128)(2,1)}, bf16[512,512]{1,0:T(8,128)(2,1)}, bf16[2048,512]{1,0:T(8,128)(2,1)}, bf16[512]{0:T(512)(128)(2,1)}) custom-call(bf16[128,512]{1,0:T(8,128)(2,1)} %get-tuple-element.15.refs_0_, bf16[512,1536]{1,0:T(8,128)(2,1)} %get-tuple-element.16.refs_1_, ...), custom_call_target="tpu_custom_call" | custom-call | tf_op jit(solution)/shard_map/hand_out/pallas_call | solution.py:477
